TPU v7x, 128 devices: a whole 4x4x4 slice. The times are simulated.
128 devices in a mesh: grp: 8 (over z_lo, y), inner: 16 (over x, z_hi, core).
Axes of the slice: x: 4, y: 4, z: 4 (z_hi: 2, z_lo: 2; z = z_hi * 2 + z_lo), core: 2. Of those that a mesh axis runs over, the one named last changes fastest.
Arguments:
- tokens: bfloat16 [2048, 8192], P('inner', 'grp'), may hold values from -170 to 170
- norm_gain: bfloat16 [8192], P('grp'), may hold values from 0.5 to 2
- gate_up_weight: bfloat16 [2, 8192, 28672], P(None, 'grp', 'inner'), may hold values from -0.0625 to 0.0625
- down_weight: bfloat16 [28672, 8192], P('inner', 'grp'), may hold values from -0.03125 to 0.03125
- student_in: bfloat16 [2048, 1024], P('grp'), may hold values from -6 to 6
- student_proj: bfloat16 [1024, 8192], P(None, 'inner'), may hold values from -0.1875 to 0.1875
Outputs:
- teacher_out: bfloat16 [2048, 8192], P('inner', 'grp')
- grad_student: float32 [2048, 1024], P('grp')
- grad_proj: float32 [1024, 8192], P(None, 'inner')
All inputs are finite; a program needn't handle non-finite values.
Results may differ from a plain program's by a relative error of at most 0.025.
Values may be sent and summed in bfloat16 or wider, within the bound.
A program may use at most 128 MiB of HBM per device.

v0:
```python
import jax
import jax.numpy as jnp
from jax import lax
from jax.sharding import PartitionSpec as P

D = 8192


def activate(gate_up):
    return (jax.nn.silu(gate_up[:, 0, :]) * gate_up[:, 1, :]).astype(jnp.bfloat16)


def shards(tokens, norm_gain, gate_up_weight, down_weight, student_in, student_proj):
    values = tokens.astype(jnp.float32)
    squares = jnp.sum(values * values, axis=1)
    row_total = lax.psum(squares, "grp")
    inverse = lax.rsqrt(row_total / D + 1e-05)
    normed = (values * inverse[:, None] * norm_gain.astype(jnp.float32)[None, :]).astype(
        jnp.bfloat16
    )
    gathered = lax.all_gather(normed, "inner", axis=0, tiled=True)
    row_block = gathered
    shares = lax.psum_scatter(
        jnp.einsum(
            "rd,kdf->rkf", row_block, gate_up_weight, preferred_element_type=jnp.float32
        ).astype(jnp.bfloat16),
        "grp",
        scatter_dimension=0,
        tiled=True,
    ).astype(jnp.float32)
    hidden = lax.all_gather(activate(shares), "grp", axis=0, tiled=True)
    row_block = hidden
    teacher_out = lax.psum_scatter(
        jnp.dot(row_block, down_weight, preferred_element_type=jnp.float32).astype(jnp.bfloat16),
        "inner",
        scatter_dimension=0,
        tiled=True,
    )
    own_rows = student_in.shape[0]
    all_columns = lax.all_gather(teacher_out, "grp", axis=1, tiled=True)
    exchanged = lax.all_to_all(all_columns, "inner", split_axis=1, concat_axis=0, tiled=True)
    target = lax.dynamic_slice_in_dim(exchanged, lax.axis_index("grp") * own_rows, own_rows, 0)
    predicted = jnp.tanh(jnp.dot(student_in, student_proj, preferred_element_type=jnp.float32))
    mismatch = predicted - target.astype(jnp.float32)
    pre_grad = (mismatch * (1.0 - predicted * predicted)).astype(jnp.bfloat16)
    input_term = lax.dot_general(
        pre_grad, student_proj, (((1,), (1,)), ((), ())), preferred_element_type=jnp.float32
    )
    grad_student = lax.psum(input_term.astype(jnp.bfloat16), "inner").astype(jnp.float32)
    weight_term = lax.dot_general(
        student_in, pre_grad, (((0,), (0,)), ((), ())), preferred_element_type=jnp.float32
    )
    grad_proj = lax.psum(weight_term.astype(jnp.bfloat16), "grp").astype(jnp.float32)
    return (teacher_out, grad_student, grad_proj)


def solution(mesh):
    return jax.shard_map(
        shards,
        mesh=mesh,
        in_specs=(
            P("inner", "grp"),
            P("grp"),
            P(None, "grp", "inner"),
            P("inner", "grp"),
            P("grp", None),
            P(None, "inner"),
        ),
        out_specs=(P("inner", "grp"), P("grp", None), P(None, "inner")),
        check_vma=False,
    )
```

profile of v0, /device:TPU:0, one launch (start us, length us, event | category | flops | bytes accessed | tf_op | source)
XLA Modules:
  0.0 746.7 jit_solution(11632876559450795353)
XLA Ops:
  7.2 0.0 copy-start
  7.2 0.0 all-gather.4.cloned.1.call-start
  7.2 0.8 convert_element_type.43
  8.0 1.1 fusion.4
  9.1 20.4 %psum.21 = f32[128]{0:T(128)S(1)} all-reduce(f32[128]{0:T(128)S(1)} %fusion.4), channel_id=1, replica_groups=mesh['grp'=8,'inner'=16] {'grp'}, use_global_device_ids=true, to_apply=%region_1.0 | all-reduce | flops 128 | bytes 1024 | tf_op jit(solution)/shard_map/psum | solution.py:16
  29.5 1.8 fusion.6
  31.3 0.0 all-gather.4.cloned.1.call-update
  31.3 0.0 reduce-scatter.3.cloned.1.call-start
  31.3 55.4 %all-gather.4.cloned.1.call-done = bf16[2048,1024]{1,0:T(8,128)(2,1)} async-done(((bf16[128,1024]{1,0:T(8,128)(2,1)}), bf16[2048,1024]{1,0:T(8,128)(2,1)}) %all-gather.4.cloned.1.call-update) | async-done | bytes 4194320 | tf_op jit(solution)/shard_map/all_gather | solution.py:21
  86.8 22.0 %convolution_convert_fusion = bf16[2048,2,1792]{2,0,1:T(8,128)(2,1)} fusion(bf16[2,1024,1792]{2,1,0:T(8,128)(2,1)} %param.8, bf16[2048,1024]{1,0:T(8,128)(2,1)} %all-gather.4.cloned.1.call-done), kind=kOutput, calls=%fused_computation | convolution fusion | flops 15039725568 | bytes 26214400 | tf_op jit(solution)/shard_map/rd,kdf->rkf/dot_general | solution.py:24
  108.8 0.0 reduce-scatter.3.cloned.1.call-update
  108.8 0.0 all-gather.6.cloned.1.call-start
  108.9 150.9 %reduce-scatter.3.cloned.1.call-done = bf16[256,2,1792]{2,0,1:T(8,128)(2,1)} async-done(((bf16[2048,2,1792]{2,0,1:T(8,128)(2,1)}), bf16[256,2,1792]{2,0,1:T(8,128)(2,1)}) %reduce-scatter.3.cloned.1.call-update) | async-done | bytes 1835024 | tf_op jit(solution)/shard_map/reduce_scatter | solution.py:23
  259.7 1.8 convert_element_type.46
  261.5 1.5 fusion.2
  263.0 0.0 all-gather.6.cloned.1.call-update
  263.0 0.0 reduce-scatter.5.cloned.1.call-start
  263.1 81.0 %all-gather.6.cloned.1.call-done = bf16[2048,1792]{1,0:T(8,128)(2,1)} async-done(((bf16[256,1792]{1,0:T(8,128)(2,1)}), bf16[2048,1792]{1,0:T(8,128)(2,1)}) %all-gather.6.cloned.1.call-update) | async-done | bytes 7340048 | tf_op jit(solution)/shard_map/all_gather | solution.py:31
  344.1 12.4 %convolution_convert_fusion.1 = bf16[2048,1024]{1,0:T(8,128)(2,1)} fusion(bf16[2048,1792]{1,0:T(8,128)(2,1)} %all-gather.6.cloned.1.call-done, bf16[1792,1024]{1,0:T(8,128)(2,1)} %param.9), kind=kOutput, calls=%fused_computation.2 | convolution fusion | flops 7518289920 | bytes 15204352 | tf_op jit(solution)/shard_map/dot_general | solution.py:34
  356.4 0.0 reduce-scatter.5.cloned.1.call-update
  356.5 0.0 all-gather.8.cloned.1.call-start
  356.5 79.3 %reduce-scatter.5.cloned.1.call-done = bf16[128,1024]{1,0:T(8,128)(2,1)} async-done(((bf16[2048,1024]{1,0:T(8,128)(2,1)}), bf16[128,1024]{1,0:T(8,128)(2,1)}) %reduce-scatter.5.cloned.1.call-update) | async-done | bytes 262160 | tf_op jit(solution)/shard_map/reduce_scatter | solution.py:33
  435.8 0.0 all-gather.8.cloned.1.call-update
  435.8 42.4 %all-gather.8.cloned.1.call-done = bf16[128,8192]{1,0:T(8,128)(2,1)} async-done(((bf16[128,1024]{1,0:T(8,128)(2,1)}), bf16[128,8192]{1,0:T(8,128)(2,1)}) %all-gather.8.cloned.1.call-update) | async-done | bytes 2097168 | tf_op jit(solution)/shard_map/all_gather | solution.py:40
  478.3 3.1 copy.15
  481.4 6.7 all-to-all-start
  488.1 0.0 all-reduce.3.cloned.1.call-start
  488.1 29.2 %all-to-all-done = bf16[128,16,512]{2,0,1:T(8,128)(2,1)S(1)} async-done(((bf16[128,16,512]{2,0,1:T(8,128)(2,1)}), bf16[128,16,512]{2,0,1:T(8,128)(2,1)S(1)}, u32[]{:S(2)}, u32[]{:S(2)}) %all-to-all-start) | async-done | bytes 2097184 | tf_op jit(solution)/shard_map/all_to_all | solution.py:41
  517.3 0.0 copy-done
  517.3 1.5 multiply_convert_fusion
  518.8 1.3 convolution_convert_fusion.3
  520.1 0.0 all-reduce.3.cloned.1.call-update
  520.1 0.0 all-reduce.5.cloned.1.call-start
  520.2 2.5 fusion.3
  522.7 0.0 all-reduce.5.cloned.1.call-update
  522.7 133.4 %all-reduce.3.cloned.1.call-done = bf16[256,1024]{1,0:T(8,128)(2,1)} async-done(((bf16[256,1024]{1,0:T(8,128)(2,1)}), bf16[256,1024]{1,0:T(8,128)(2,1)}) %all-reduce.3.cloned.1.call-update) | async-done | bytes 524304 | tf_op jit(solution)/shard_map/psum | solution.py:49
  656.1 2.1 convert_element_type.52
  658.2 79.1 %all-reduce.5.cloned.1.call-done = bf16[1024,512]{0,1:T(8,128)(2,1)} async-done(((bf16[1024,512]{0,1:T(8,128)(2,1)}), bf16[1024,512]{0,1:T(8,128)(2,1)}) %all-reduce.5.cloned.1.call-update) | async-done | bytes 1048592 | tf_op jit(solution)/shard_map/psum | solution.py:53
  737.3 2.6 copy.12
  (1 shorter events, 0.0 us)
Async XLA Ops:
  7.2 510.1 %copy-start = (bf16[1024,512]{1,0:T(8,128)(2,1)S(1)}, bf16[1024,512]{1,0:T(8,128)(2,1)}, u32[]{:S(2)}) copy-start(bf16[1024,512]{1,0:T(8,128)(2,1)} %param.11) | copy-start | bytes 3145732
  7.2 79.6 %all-gather.4.cloned.1.call-start = ((), (), s32[]{:S(2)}) async-start(), calls=%async_computation.3 | async-start | bytes 4456448 | tf_op jit(solution)/shard_map/all_gather | solution.py:21
  31.3 228.5 %reduce-scatter.3.cloned.1.call-start = ((), (), s32[]{:S(2)}) async-start(), calls=%async_computation.4 | async-start | bytes 16515072 | tf_op jit(solution)/shard_map/reduce_scatter | solution.py:23
  108.8 235.3 %all-gather.6.cloned.1.call-start = ((), (), s32[]{:S(2)}) async-start(), calls=%async_computation.5 | async-start | bytes 8257536 | tf_op jit(solution)/shard_map/all_gather | solution.py:31
  263.0 172.8 %reduce-scatter.5.cloned.1.call-start = ((), (), s32[]{:S(2)}) async-start(), calls=%async_computation.6 | async-start | bytes 4456448 | tf_op jit(solution)/shard_map/reduce_scatter | solution.py:33
  356.5 121.8 %all-gather.8.cloned.1.call-start = ((), (), s32[]{:S(2)}) async-start(), calls=%async_computation.7 | async-start | bytes 2359296 | tf_op jit(solution)/shard_map/all_gather | solution.py:40
  481.4 35.9 %all-to-all-start = ((bf16[128,16,512]{2,0,1:T(8,128)(2,1)}), bf16[128,16,512]{2,0,1:T(8,128)(2,1)S(1)}, u32[]{:S(2)}, u32[]{:S(2)}) async-start(bf16[128,16,512]{2,0,1:T(8,128)(2,1)} %bitcast.30), calls=%async_computation.2 | async-start | bytes 4194304 | tf_op jit(solution)/shard_map/all_to_all | solution.py:41
  488.1 168.0 %all-reduce.3.cloned.1.call-start = ((), (), s32[]{:S(2)}) async-start(), calls=%async_computation.8 | async-start | bytes 1048576 | tf_op jit(solution)/shard_map/psum | solution.py:49
  520.1 217.2 %all-reduce.5.cloned.1.call-start = ((), (), s32[]{:S(2)}) async-start(), calls=%async_computation.9 | async-start | bytes 2097152 | tf_op jit(solution)/shard_map/psum | solution.py:53
Sparse Core Ops, SparseCore 0:
  31.4 55.3 all-gather.3
  108.9 150.7 reduce-scatter.2
  263.1 80.8 all-gather.5
  356.6 79.1 reduce-scatter.4
  438.0 40.2 all-gather.7
  520.3 135.7 all-reduce.2
  659.1 78.1 all-reduce.4
where the time goes:
time: 747 us
  waiting for transfers between devices  651 us (87%)
  matrix products  39.7 us (5%)
  blocking collectives  20.4 us (3%)
  between operations  14.2 us (2%)
  other arithmetic  9 us (1%)
    reduce_scatter x1, waiting for transfers between devices, shards(): lax.psum_scatter(jnp.einsum('rd,kdf->rkf', row_block, gate_up_weight, pre...  151 us
    psum x1, waiting for transfers between devices, shards(): lax.psum(input_term.astype(jnp.bfloat16), 'inner').astype(jnp.float32)  133 us
    all_gather x1, waiting for transfers between devices, shards(): hidden = lax.all_gather(activate(shares), 'grp', axis=0, tiled=True)  81 us
    reduce_scatter x1, waiting for transfers between devices, shards(): lax.psum_scatter(jnp.dot(row_block, down_weight, preferred_element_type=j...  79.3 us
    psum x1, waiting for transfers between devices, shards(): lax.psum(weight_term.astype(jnp.bfloat16), 'grp').astype(jnp.float32)  79.1 us
    all_gather x1, waiting for transfers between devices, shards(): gathered = lax.all_gather(normed, 'inner', axis=0, tiled=True)  55.4 us
    all_gather x1, waiting for transfers between devices, shards(): all_columns = lax.all_gather(teacher_out, 'grp', axis=1, tiled=True)  42.4 us
    all_to_all x1, waiting for transfers between devices, shards(): lax.all_to_all(all_columns, 'inner', split_axis=1, concat_axis=0, tiled=T...  29.2 us
  transfers between devices with their start and end apart: 8, of which 8 were waited for; matrix products, arithmetic and copies ran while one was open for 1% of the time, Pallas kernels for 0%

commit v1 on v0

--- a/solution.py
+++ b/solution.py
@@ -50,7 +50,9 @@
     weight_term = lax.dot_general(
         student_in, pre_grad, (((0,), (0,)), ((), ())), preferred_element_type=jnp.float32
     )
-    grad_proj = lax.psum(weight_term.astype(jnp.bfloat16), "grp").astype(jnp.float32)
+    grad_proj = jnp.sum(lax.all_gather(weight_term.astype(jnp.bfloat16), "grp"), axis=0).astype(
+        jnp.float32
+    )
     return (teacher_out, grad_student, grad_proj)
 
 

time: 747 us -> 788 us (1.055)
  local copies, waits for them, and re-layouts: 5.71 us -> 21.1 us
  waiting for transfers between devices: 651 us -> 665 us
  other arithmetic: 9 us -> 19.9 us
    all_gather x0 -> x1, waiting for transfers between devices: none -> 93 us  [shards(): lax.all_gather(weight_term.astype(jnp.bfloat16), 'grp')]
    psum x1 -> x0, waiting for transfers between devices: 79.1 us -> none  [shards(): lax.psum(weight_term.astype(jnp.bfloat16), 'grp').astype(jnp.float32)]
    unnamed x3 -> x4, local copies, waits for them, and re-layouts: 2.58 us -> 18 us
    reduce_sum x0 -> x1, other arithmetic: none -> 10.9 us  [shards(): jnp.sum(lax.all_gather(weight_term.astype(jnp.bfloat16), 'grp'), axis=0)]
where the time goes in v1:
time: 788 us; the launch traced here: 787 us
  waiting for transfers between devices  665 us (84%)
  matrix products  39.6 us (5%)
  local copies, waits for them, and re-layouts  21.1 us (3%)
  blocking collectives  20.4 us (3%)
  other arithmetic  19.9 us (3%)
  between operations  14.2 us (2%)
    reduce_scatter x1, waiting for transfers between devices, shards(): lax.psum_scatter(jnp.einsum('rd,kdf->rkf', row_block, gate_up_weight, pre...  151 us
    psum x1, waiting for transfers between devices, shards(): lax.psum(input_term.astype(jnp.bfloat16), 'inner').astype(jnp.float32)  133 us
    all_gather x1, waiting for transfers between devices, shards(): lax.all_gather(weight_term.astype(jnp.bfloat16), 'grp')  93 us
    all_gather x1, waiting for transfers between devices, shards(): hidden = lax.all_gather(activate(shares), 'grp', axis=0, tiled=True)  81 us
    reduce_scatter x1, waiting for transfers between devices, shards(): lax.psum_scatter(jnp.dot(row_block, down_weight, preferred_element_type=j...  79.3 us
    all_gather x1, waiting for transfers between devices, shards(): gathered = lax.all_gather(normed, 'inner', axis=0, tiled=True)  55.4 us
    all_gather x1, waiting for transfers between devices, shards(): all_columns = lax.all_gather(teacher_out, 'grp', axis=1, tiled=True)  42.4 us
    all_to_all x1, waiting for transfers between devices, shards(): lax.all_to_all(all_columns, 'inner', split_axis=1, concat_axis=0, tiled=T...  29.2 us
  transfers between devices with their start and end apart: 8, of which 8 were waited for; matrix products, arithmetic and copies ran while one was open for 1% of the time, Pallas kernels for 0%

profile of v1, /device:TPU:0, one launch (start us, length us, event | category | flops | bytes accessed | tf_op | source)
XLA Modules:
  0.0 786.9 jit_solution(13549106780632552079)
XLA Ops:
  7.2 0.0 copy-start
  7.2 0.0 all-gather.6.cloned.1.call-start
  7.2 0.8 convert_element_type.45
  8.0 1.1 fusion.4
  9.1 20.4 %psum.14 = f32[128]{0:T(128)S(1)} all-reduce(f32[128]{0:T(128)S(1)} %fusion.4), channel_id=1, replica_groups=mesh['grp'=8,'inner'=16] {'grp'}, use_global_device_ids=true, to_apply=%region_1.0 | all-reduce | flops 128 | bytes 1024 | tf_op jit(solution)/shard_map/psum | solution.py:16
  29.5 1.8 fusion.6
  31.3 0.0 all-gather.6.cloned.1.call-update
  31.3 0.0 reduce-scatter.3.cloned.1.call-start
  31.3 55.4 %all-gather.6.cloned.1.call-done = bf16[2048,1024]{1,0:T(8,128)(2,1)} async-done(((bf16[128,1024]{1,0:T(8,128)(2,1)}), bf16[2048,1024]{1,0:T(8,128)(2,1)}) %all-gather.6.cloned.1.call-update) | async-done | bytes 4194320 | tf_op jit(solution)/shard_map/all_gather | solution.py:21
  86.8 22.0 %convolution_convert_fusion = bf16[2048,2,1792]{2,0,1:T(8,128)(2,1)} fusion(bf16[2,1024,1792]{2,1,0:T(8,128)(2,1)} %param.8, bf16[2048,1024]{1,0:T(8,128)(2,1)} %all-gather.6.cloned.1.call-done), kind=kOutput, calls=%fused_computation | convolution fusion | flops 15039725568 | bytes 26214400 | tf_op jit(solution)/shard_map/rd,kdf->rkf/dot_general | solution.py:24
  108.8 0.0 reduce-scatter.3.cloned.1.call-update
  108.8 0.0 all-gather.8.cloned.1.call-start
  108.8 150.9 %reduce-scatter.3.cloned.1.call-done = bf16[256,2,1792]{2,0,1:T(8,128)(2,1)} async-done(((bf16[2048,2,1792]{2,0,1:T(8,128)(2,1)}), bf16[256,2,1792]{2,0,1:T(8,128)(2,1)}) %reduce-scatter.3.cloned.1.call-update) | async-done | bytes 1835024 | tf_op jit(solution)/shard_map/reduce_scatter | solution.py:23
  259.8 1.8 convert_element_type.48
  261.5 1.5 fusion.2
  263.0 0.0 all-gather.8.cloned.1.call-update
  263.0 0.0 reduce-scatter.5.cloned.1.call-start
  263.1 81.0 %all-gather.8.cloned.1.call-done = bf16[2048,1792]{1,0:T(8,128)(2,1)} async-done(((bf16[256,1792]{1,0:T(8,128)(2,1)}), bf16[2048,1792]{1,0:T(8,128)(2,1)}) %all-gather.8.cloned.1.call-update) | async-done | bytes 7340048 | tf_op jit(solution)/shard_map/all_gather | solution.py:31
  344.1 12.4 %convolution_convert_fusion.1 = bf16[2048,1024]{1,0:T(8,128)(2,1)} fusion(bf16[2048,1792]{1,0:T(8,128)(2,1)} %all-gather.8.cloned.1.call-done, bf16[1792,1024]{1,0:T(8,128)(2,1)} %param.9), kind=kOutput, calls=%fused_computation.3 | convolution fusion | flops 7518289920 | bytes 15204352 | tf_op jit(solution)/shard_map/dot_general | solution.py:34
  356.5 0.0 reduce-scatter.5.cloned.1.call-update
  356.5 0.0 all-gather.10.cloned.1.call-start
  356.5 79.3 %reduce-scatter.5.cloned.1.call-done = bf16[128,1024]{1,0:T(8,128)(2,1)} async-done(((bf16[2048,1024]{1,0:T(8,128)(2,1)}), bf16[128,1024]{1,0:T(8,128)(2,1)}) %reduce-scatter.5.cloned.1.call-update) | async-done | bytes 262160 | tf_op jit(solution)/shard_map/reduce_scatter | solution.py:33
  435.8 0.0 all-gather.10.cloned.1.call-update
  435.9 42.4 %all-gather.10.cloned.1.call-done = bf16[128,8192]{1,0:T(8,128)(2,1)} async-done(((bf16[128,1024]{1,0:T(8,128)(2,1)}), bf16[128,8192]{1,0:T(8,128)(2,1)}) %all-gather.10.cloned.1.call-update) | async-done | bytes 2097168 | tf_op jit(solution)/shard_map/all_gather | solution.py:40
  478.3 3.1 copy.15
  481.4 6.7 all-to-all-start
  488.1 0.0 all-reduce.2.cloned.1.call-start
  488.1 29.2 %all-to-all-done = bf16[128,16,512]{2,0,1:T(8,128)(2,1)S(1)} async-done(((bf16[128,16,512]{2,0,1:T(8,128)(2,1)}), bf16[128,16,512]{2,0,1:T(8,128)(2,1)S(1)}, u32[]{:S(2)}, u32[]{:S(2)}) %all-to-all-start) | async-done | bytes 2097184 | tf_op jit(solution)/shard_map/all_to_all | solution.py:41
  517.3 0.0 copy-done
  517.3 1.5 multiply_convert_fusion
  518.8 1.3 convolution_convert_fusion.3
  520.1 0.0 all-reduce.2.cloned.1.call-update
  520.1 0.2 all-gather.12.cloned.1.call-start
  520.4 2.5 fusion.3
  522.8 0.0 all-gather.12.cloned.1.call-update
  522.9 133.2 %all-reduce.2.cloned.1.call-done = bf16[256,1024]{1,0:T(8,128)(2,1)} async-done(((bf16[256,1024]{1,0:T(8,128)(2,1)}), bf16[256,1024]{1,0:T(8,128)(2,1)}) %all-reduce.2.cloned.1.call-update) | async-done | bytes 524304 | tf_op jit(solution)/shard_map/psum | solution.py:49
  656.1 2.1 convert_element_type.54
  658.2 93.0 %all-gather.12.cloned.1.call-done = bf16[8192,512]{0,1:T(8,128)(2,1)} async-done(((bf16[1024,512]{0,1:T(8,128)(2,1)}), bf16[8192,512]{0,1:T(8,128)(2,1)}) %all-gather.12.cloned.1.call-update) | async-done | bytes 8388624 | tf_op jit(solution)/shard_map/all_gather | solution.py:53
  751.2 16.3 %copy.13 = bf16[64,8,8,1024]{3,2,1,0:T(8,128)(2,1)} copy(bf16[64,8,8,1024]{3,1,2,0:T(8,128)(2,1)} %bitcast.36) | data formatting | bytes 16777216
  767.6 10.9 %bitcast_reduce_fusion = bf16[1024,512]{0,1:T(8,128)(2,1)S(1)} fusion(bf16[64,8,8,1024]{3,2,1,0:T(8,128)(2,1)} %copy.13), kind=kLoop, calls=%fused_computation.1 | loop fusion | flops 3670016 | bytes 9437184 | tf_op jit(solution)/shard_map/reduce_sum | solution.py:53
  778.5 1.6 copy.11
  (1 shorter events, 0.0 us)
Async XLA Ops:
  7.2 510.1 %copy-start = (bf16[1024,512]{1,0:T(8,128)(2,1)S(1)}, bf16[1024,512]{1,0:T(8,128)(2,1)}, u32[]{:S(2)}) copy-start(bf16[1024,512]{1,0:T(8,128)(2,1)} %param.11) | copy-start | bytes 3145732
  7.2 79.6 %all-gather.6.cloned.1.call-start = ((), (), s32[]{:S(2)}) async-start(), calls=%async_computation.3 | async-start | bytes 4456448 | tf_op jit(solution)/shard_map/all_gather | solution.py:21
  31.3 228.5 %reduce-scatter.3.cloned.1.call-start = ((), (), s32[]{:S(2)}) async-start(), calls=%async_computation.4 | async-start | bytes 16515072 | tf_op jit(solution)/shard_map/reduce_scatter | solution.py:23
  108.8 235.3 %all-gather.8.cloned.1.call-start = ((), (), s32[]{:S(2)}) async-start(), calls=%async_computation.5 | async-start | bytes 8257536 | tf_op jit(solution)/shard_map/all_gather | solution.py:31
  263.0 172.8 %reduce-scatter.5.cloned.1.call-start = ((), (), s32[]{:S(2)}) async-start(), calls=%async_computation.6 | async-start | bytes 4456448 | tf_op jit(solution)/shard_map/reduce_scatter | solution.py:33
  356.5 121.8 %all-gather.10.cloned.1.call-start = ((), (), s32[]{:S(2)}) async-start(), calls=%async_computation.7 | async-start | bytes 2359296 | tf_op jit(solution)/shard_map/all_gather | solution.py:40
  481.4 35.9 %all-to-all-start = ((bf16[128,16,512]{2,0,1:T(8,128)(2,1)}), bf16[128,16,512]{2,0,1:T(8,128)(2,1)S(1)}, u32[]{:S(2)}, u32[]{:S(2)}) async-start(bf16[128,16,512]{2,0,1:T(8,128)(2,1)} %bitcast.35), calls=%async_computation.2 | async-start | bytes 4194304 | tf_op jit(solution)/shard_map/all_to_all | solution.py:41
  488.1 168.0 %all-reduce.2.cloned.1.call-start = ((), (), s32[]{:S(2)}) async-start(), calls=%async_computation.8 | async-start | bytes 1048576 | tf_op jit(solution)/shard_map/psum | solution.py:49
  520.1 231.1 %all-gather.12.cloned.1.call-start = ((), (), s32[]{:S(2)}) async-start(), calls=%async_computation.9 | async-start | bytes 9437184 | tf_op jit(solution)/shard_map/all_gather | solution.py:53
Sparse Core Ops, SparseCore 0:
  31.4 55.3 all-gather.5
  108.9 150.7 reduce-scatter.2
  263.1 80.8 all-gather.7
  356.6 79.1 reduce-scatter.4
  438.0 40.2 all-gather.9
  520.3 135.7 all-reduce.1
  658.3 92.9 all-gather.11
